TPU v7x, 256 devices: a whole 4x4x8 slice. The times are simulated.
256 devices in a mesh: dp: 2 (over core), dom: 128 (over y, z, x).
Axes of the slice: x: 4, y: 4, z: 8, core: 2. Of those that a mesh axis runs over, the one named last changes fastest.
Arguments:
- features: bfloat16 [2, 49152, 512], P('dp', 'dom'), may hold values from -12 to 12
- tile_mask: int32 [2, 384, 18], P('dp', 'dom'), may hold values from 0 to 1, as said below
- cotangent: bfloat16 [2, 49152, 512], P('dp', 'dom'), may hold values from -6 to 6
- w_query: bfloat16 [512, 512], replicated, may hold values from -1 to 1
- w_key: bfloat16 [512, 512], replicated, may hold values from -1 to 1
- w_value: bfloat16 [512, 512], replicated, may hold values from -0.25 to 0.25
- w_out: bfloat16 [512, 512], replicated, may hold values from -0.25 to 0.25
Outputs:
- attended: bfloat16 [2, 49152, 512], P('dp', 'dom')
- grad_features: bfloat16 [2, 49152, 512], P('dp', 'dom')
- grad_query: float32 [512, 512], replicated
- grad_key: float32 [512, 512], replicated
- grad_value: float32 [512, 512], replicated
- grad_out: float32 [512, 512], replicated
Inputs may be any that keep to these rules, and one draw needn't show every extreme that they name: `tile_mask`: 0 or 1; the share of ones differs between tile groups, from about a quarter to all.
All inputs are finite; a program needn't handle non-finite values.
Results may differ from a plain program's by a relative error of at most 0.023.
Values may be sent and summed in bfloat16 or wider, within the bound.
A program may use at most 128 MiB of HBM per device.

v0:
```python
import jax
import jax.numpy as jnp
from jax import lax
from jax.sharding import PartitionSpec as P

HEADS = 8
HEAD_DIM = 64
TILE = 128
TILE_DEV = 3
NB = 3
CANDT = 18


def with_halo(block, sides, width):
    for axis, dim in sides:
        count = lax.axis_size(axis)
        forward = [(i, i + 1) for i in range(count - 1)]
        forward.append((count - 1, 0))
        backward = [(target, source) for source, target in forward]
        low = lax.ppermute(
            lax.slice_in_dim(block, block.shape[dim] - width, None, axis=dim), axis, forward
        )
        high = lax.ppermute(lax.slice_in_dim(block, 0, width, axis=dim), axis, backward)
        block = jnp.concatenate([low, block, high], axis=dim)
    return block


def from_partner(value, axis, distance):
    mask = 2**distance
    pairs = [(source, source ^ mask) for source in range(lax.axis_size(axis))]
    return lax.ppermute(value, axis, pairs)


def candidate_blocks(block):
    block_rows = block.shape[0]
    near = with_halo(block, (("dom", 0),), block_rows)
    pieces = [block, near[:block_rows], near[2 * block_rows :]]
    levels = lax.axis_size("dom").bit_length() - 1
    for bit_step in range(NB):
        pieces.append(from_partner(block, "dom", levels - 1 - bit_step))
    return pieces


def returned_sum(grad_parts):
    block_rows = grad_parts.shape[1]
    outgoing = jnp.concatenate([grad_parts[1], grad_parts[2]], 0)
    returned = with_halo(outgoing, (("dom", 0),), block_rows)
    summed = grad_parts[0] + returned[:block_rows] + returned[3 * block_rows :]
    levels = lax.axis_size("dom").bit_length() - 1
    for bit_step in range(NB):
        summed = summed + from_partner(grad_parts[3 + bit_step], "dom", levels - 1 - bit_step)
    return summed


def joined(stacked_parts, width_all):
    return jnp.transpose(stacked_parts, (1, 0, 2)).reshape(stacked_parts.shape[1], width_all)


def per_device(features, tile_mask, cotangent, w_query, w_key, w_value, w_out):
    node_rows = features[0]
    block_rows = node_rows.shape[0]
    width_all = node_rows.shape[1]
    highest = lax.Precision.HIGHEST
    factor = HEAD_DIM ** (-0.5)
    w_both = jnp.concatenate([w_key, w_value], 1)
    q_rows = jnp.dot(node_rows, w_query, preferred_element_type=jnp.float32).astype(jnp.bfloat16)
    kv_rows = jnp.dot(node_rows, w_both, preferred_element_type=jnp.float32).astype(jnp.bfloat16)
    cand_kv = jnp.concatenate(candidate_blocks(kv_rows), 0)
    key_count = cand_kv.shape[0]
    keys_all = cand_kv[:, :width_all]
    values_all = cand_kv[:, width_all:]
    own_tile = jnp.arange(CANDT)[None, :] == jnp.arange(TILE_DEV)[:, None]
    live_tiles = (tile_mask[0] == 1) | own_tile
    masking = jnp.where(live_tiles, 0.0, -1e30).astype(jnp.float32)
    cot_rows = cotangent[0]
    grad_o = jnp.dot(cot_rows, w_out.T, preferred_element_type=jnp.float32).astype(jnp.bfloat16)
    pair_cols = 2 * HEAD_DIM

    def head_pair(pair_index):
        col_start = pair_index * pair_cols
        q_pair = lax.dynamic_slice_in_dim(q_rows, col_start, pair_cols, 1).reshape(
            block_rows, 2, HEAD_DIM
        )
        k_pair = lax.dynamic_slice_in_dim(keys_all, col_start, pair_cols, 1).reshape(
            key_count, 2, HEAD_DIM
        )
        v_pair = lax.dynamic_slice_in_dim(values_all, col_start, pair_cols, 1).reshape(
            key_count, 2, HEAD_DIM
        )
        g_pair = lax.dynamic_slice_in_dim(grad_o, col_start, pair_cols, 1).reshape(
            block_rows, 2, HEAD_DIM
        )
        scores = (
            jnp.einsum("rhd,chd->hrc", q_pair, k_pair, preferred_element_type=jnp.float32) * factor
        )
        scores = scores.reshape(2, TILE_DEV, TILE, CANDT, TILE) + masking[None, :, None, :, None]
        scores = scores.reshape(2, block_rows, key_count)
        row_max = jnp.max(scores, axis=2, keepdims=True)
        exp_vals = jnp.exp(scores - row_max)
        prob_f32 = exp_vals / jnp.sum(exp_vals, axis=2, keepdims=True)
        prob_bf = prob_f32.astype(jnp.bfloat16)
        out_pair = jnp.einsum(
            "hrc,chd->rhd", prob_bf, v_pair, preferred_element_type=jnp.float32
        ).astype(jnp.bfloat16)
        grad_prob = jnp.einsum("rhd,chd->hrc", g_pair, v_pair, preferred_element_type=jnp.float32)
        row_delta = jnp.einsum(
            "rhd,rhd->hr", g_pair.astype(jnp.float32), out_pair.astype(jnp.float32)
        )
        grad_score = (prob_f32 * (grad_prob - row_delta[:, :, None]) * factor).astype(jnp.bfloat16)
        gq_pair = jnp.einsum(
            "hrc,chd->rhd", grad_score, k_pair, preferred_element_type=jnp.float32
        ).reshape(block_rows, pair_cols)
        gk_pair = jnp.einsum(
            "hrc,rhd->chd", grad_score, q_pair, preferred_element_type=jnp.float32
        ).reshape(key_count, pair_cols)
        gv_pair = jnp.einsum(
            "hrc,rhd->chd", prob_bf, g_pair, preferred_element_type=jnp.float32
        ).reshape(key_count, pair_cols)
        return (out_pair.reshape(block_rows, pair_cols), gq_pair, gk_pair, gv_pair)

    stacked = lax.map(head_pair, jnp.arange(HEADS // 2, dtype=jnp.int32))
    out_rows = joined(stacked[0], width_all)
    grad_q = joined(stacked[1], width_all)
    grad_k = joined(stacked[2], width_all)
    grad_v = joined(stacked[3], width_all)
    attended = jnp.dot(out_rows, w_out, preferred_element_type=jnp.float32).astype(jnp.bfloat16)
    grad_parts = jnp.concatenate([grad_k, grad_v], 1).reshape(3 + NB, block_rows, 2 * width_all)
    w_both32 = w_both.astype(jnp.float32)
    rows_f32 = node_rows.astype(jnp.float32)
    own_grad = returned_sum(grad_parts)
    kv_dx = jnp.dot(own_grad, w_both32.T, precision=highest)
    g_both = jnp.dot(rows_f32.T, own_grad, precision=highest)
    grad_x = jnp.dot(grad_q, w_query.astype(jnp.float32).T, precision=highest) + kv_dx
    g_query = jnp.dot(rows_f32.T, grad_q, precision=highest)
    g_out = jnp.dot(out_rows.T, cot_rows, preferred_element_type=jnp.float32)
    g_query, g_key, g_value, g_out = lax.psum(
        (g_query, g_both[:, :width_all], g_both[:, width_all:], g_out), ("dp", "dom")
    )
    return (attended[None], grad_x.astype(jnp.bfloat16)[None], g_query, g_key, g_value, g_out)


def solution(mesh):
    in_specs = (
        P("dp", "dom", None),
        P("dp", "dom", None),
        P("dp", "dom", None),
        P(),
        P(),
        P(),
        P(),
    )
    out_specs = (P("dp", "dom", None), P("dp", "dom", None), P(), P(), P(), P())
    return jax.shard_map(
        per_device, mesh=mesh, in_specs=in_specs, out_specs=out_specs, check_vma=False
    )
```

profile of v0, /device:TPU:1, one launch (start us, length us, event | category | flops | bytes accessed | tf_op | source)
XLA Modules:
  0.0 601.6 jit_solution(1646686012757670933)
XLA Ops:
  10.6 2.7 constant_dynamic-update-slice_fusion.11
  13.3 7.7 %collective-permute-start.4 = (bf16[384,1024]{1,0:T(8,128)(2,1)}, bf16[384,1024]{1,0:T(8,128)(2,1)S(1)}, u32[]{:S(2)}, u32[]{:S(2)}) collective-permute-start(bf16[384,1024]{1,0:T(8,128)(2,1)} %get-tuple-element.146), channel_id=1, source_target_pairs={{0,16},{1,17},{2,18},{3,19},{4,20},{5,21},{6,22},{7,23},{8,24},{9,... | collective-permute-start | bytes 2359304 | tf_op jit(solution)/shard_map/ppermute | solution.py:31
  22.4 2.6 collective-permute-start.2
  27.6 49.6 %collective-permute-done = bf16[384,1024]{1,0:T(8,128)(2,1)} collective-permute-done((bf16[384,1024]{1,0:T(8,128)(2,1)}, bf16[384,1024]{1,0:T(8,128)(2,1)}, u32[]{:S(2)}, u32[]{:S(2)}) %collective-permute-start) | collective-permute-done | bytes 786464 | tf_op jit(solution)/shard_map/ppermute | solution.py:20
  77.1 2.1 constant_dynamic-update-slice_fusion.10
  79.2 2.1 constant_dynamic-update-slice_fusion.9
  81.3 2.1 constant_dynamic-update-slice_fusion.8
  83.4 2.1 constant_dynamic-update-slice_fusion.7
  86.4 4.8 fusion.33
  91.2 110.8 %while.16 = (s32[]{:T(128)}, bf16[4,384,128]{1,2,0:T(8,128)(2,1)}, f32[4,384,128]{1,2,0:T(8,128)}, f32[4,2304,128]{1,2,0:T(8,128)}, f32[4,2304,128]{1,2,0:T(8,12...) while((s32[]{:T(128)}, bf16[4,384,128]{1,2,0:T(8,128)(2,1)}, ...), condition=%wide.region_3.4_spmd, body=%wide.region_0.3_spmd.sunk | while | flops 1378665984 | bytes 104414744 | solution.py:121
  95.9 2.5 copy.50
  98.4 7.1 %fusion.93 = (f32[2,384]{1,0:T(2,128)S(1)}, f32[2,384,2304]{2,1,0:T(8,128)}) fusion(f32[384,2304]{1,0:T(8,128)} %bitcast.143, bf16[384,2,64]{0,2,1:T(8,128)(2,1)S(1)} %bitcast.150, bf16[2304,2,64]{0,2,1:T(8,128)(2,1)S(1)} %bitcast.144), kind=kOutput, calls=%fused_computation.74.clone.1 | convolution fusion | flops 233572608 | bytes 11308032 | tf_op jit(solution)/shard_map/while/body/eval_jaxpr/sub | solution.py:99
  105.5 3.8 fusion.94
  123.7 2.5 copy.50
  126.2 7.1 %fusion.93 = (f32[2,384]{1,0:T(2,128)S(1)}, f32[2,384,2304]{2,1,0:T(8,128)}) fusion(f32[384,2304]{1,0:T(8,128)} %bitcast.143, bf16[384,2,64]{0,2,1:T(8,128)(2,1)S(1)} %bitcast.150, bf16[2304,2,64]{0,2,1:T(8,128)(2,1)S(1)} %bitcast.144), kind=kOutput, calls=%fused_computation.74.clone.1 | convolution fusion | flops 233572608 | bytes 11308032 | tf_op jit(solution)/shard_map/while/body/eval_jaxpr/sub | solution.py:99
  133.3 3.8 fusion.94
  151.4 2.5 copy.50
  153.9 7.1 %fusion.93 = (f32[2,384]{1,0:T(2,128)S(1)}, f32[2,384,2304]{2,1,0:T(8,128)}) fusion(f32[384,2304]{1,0:T(8,128)} %bitcast.143, bf16[384,2,64]{0,2,1:T(8,128)(2,1)S(1)} %bitcast.150, bf16[2304,2,64]{0,2,1:T(8,128)(2,1)S(1)} %bitcast.144), kind=kOutput, calls=%fused_computation.74.clone.1 | convolution fusion | flops 233572608 | bytes 11308032 | tf_op jit(solution)/shard_map/while/body/eval_jaxpr/sub | solution.py:99
  161.0 3.8 fusion.94
  179.1 2.5 copy.50
  181.6 7.1 %fusion.93 = (f32[2,384]{1,0:T(2,128)S(1)}, f32[2,384,2304]{2,1,0:T(8,128)}) fusion(f32[384,2304]{1,0:T(8,128)} %bitcast.143, bf16[384,2,64]{0,2,1:T(8,128)(2,1)S(1)} %bitcast.150, bf16[2304,2,64]{0,2,1:T(8,128)(2,1)S(1)} %bitcast.144), kind=kOutput, calls=%fused_computation.74.clone.1 | convolution fusion | flops 233572608 | bytes 11308032 | tf_op jit(solution)/shard_map/while/body/eval_jaxpr/sub | solution.py:99
  188.6 3.8 fusion.94
  202.0 5.9 fusion.16
  208.0 6.9 %collective-permute-start.6 = (f32[384,1024]{0,1:T(8,128)}, f32[384,1024]{0,1:T(8,128)S(1)}, u32[]{:S(2)}, u32[]{:S(2)}) collective-permute-start(f32[384,1024]{0,1:T(8,128)} %get-tuple-element.137), channel_id=1, source_target_pairs={{1,0},{2,1},{3,2},{4,3},{5,4},{6,5},{7,6},{8,7},{9,8},{10,9},{11,1... | collective-permute-start | bytes 4718600 | tf_op jit(solution)/shard_map/ppermute | solution.py:23
  214.9 3.4 collective-permute-start.9
  220.2 2.0 convolution_bitcast_fusion.1
  222.1 94.4 %collective-permute-done.5 = f32[384,1024]{0,1:T(8,128)S(1)} collective-permute-done((f32[384,1024]{0,1:T(8,128)}, f32[384,1024]{0,1:T(8,128)S(1)}, u32[]{:S(2)}, u32[]{:S(2)}) %collective-permute-start.5) | collective-permute-done | bytes 1572896 | tf_op jit(solution)/shard_map/ppermute | solution.py:20
  321.6 2.7 fusion.38
  324.3 3.4 fusion.21
  327.7 259.5 %all-reduce.3.cloned.1.call-done = (f32[512,512]{0,1:T(8,128)}, f32[512,512]{0,1:T(8,128)}, f32[512,512]{0,1:T(8,128)}, f32[512,512]{1,0:T(8,128)}) async-done(((f32[512,512]{0,1:T(8,128)}, f32[512,512]{0,1:T(8,128)}, f32[512,512]{0,1:T(8,128)}, f32[512,512]{1,0:T(8,128)}), (f32[512,512]{0,1:T(8,128)}, f32[512,512]{0,1:T(8,128)}, f32[512,512]{0,1:T(8,128)}, ...) | async-done | bytes 4194320 | tf_op jit(solution)/shard_map/psum | solution.py:136
  587.2 2.7 copy.24
  589.9 2.5 copy.25
  (165 shorter events, 71.3 us)
Async XLA Ops:
  7.2 20.0 %copy-start = (bf16[512,512]{1,0:T(8,128)(2,1)S(1)}, bf16[512,512]{1,0:T(8,128)(2,1)}, u32[]{:S(2)}) copy-start(bf16[512,512]{1,0:T(8,128)(2,1)} %param.15) | copy-start | bytes 1572868
  7.2 19.5 %copy-start.4 = (bf16[1,384,512]{2,1,0:T(8,128)(2,1)S(1)}, bf16[1,384,512]{2,1,0:T(8,128)(2,1)}, u32[]{:S(2)}) copy-start(bf16[1,384,512]{2,1,0:T(8,128)(2,1)} %param.9) | copy-start | bytes 1179652
  7.2 19.5 %copy-start.6 = (bf16[512,512]{1,0:T(8,128)(2,1)S(1)}, bf16[512,512]{1,0:T(8,128)(2,1)}, u32[]{:S(2)}) copy-start(bf16[512,512]{1,0:T(8,128)(2,1)} %param.12) | copy-start | bytes 1572868
  7.2 19.9 %copy-start.14 = (s32[1,3,18]{2,0,1:T(1,128)S(1)}, s32[1,3,18]{2,0,1:T(1,128)}, u32[]{:S(2)}) copy-start(s32[1,3,18]{2,0,1:T(1,128)} %param.10) | copy-start | bytes 652
  7.2 19.9 %copy-start.9 = (bf16[1,384,512]{2,1,0:T(8,128)(2,1)S(1)}, bf16[1,384,512]{2,1,0:T(8,128)(2,1)}, u32[]{:S(2)}) copy-start(bf16[1,384,512]{2,1,0:T(8,128)(2,1)} %param.11) | copy-start | bytes 1179652
  7.2 580.0 %all-reduce.3.cloned.1.call-start = ((), (), s32[]{:S(2)}) async-start(), calls=%async_computation | async-start | bytes 8388608 | tf_op jit(solution)/shard_map/psum | solution.py:136
  13.3 72.1 %collective-permute-start.4 = (bf16[384,1024]{1,0:T(8,128)(2,1)}, bf16[384,1024]{1,0:T(8,128)(2,1)S(1)}, u32[]{:S(2)}, u32[]{:S(2)}) collective-permute-start(bf16[384,1024]{1,0:T(8,128)(2,1)} %get-tuple-element.146), channel_id=1, source_target_pairs={{0,16},{1,17},{2,18},{3,19},{4,20},{5,21},{6,22},{7,23},{8,24},{9,... | collective-permute-start | bytes 2359304 | tf_op jit(solution)/shard_map/ppermute | solution.py:31
  21.1 62.3 %collective-permute-start.3 = (bf16[384,1024]{1,0:T(8,128)(2,1)}, bf16[384,1024]{1,0:T(8,128)(2,1)}, u32[]{:S(2)}, u32[]{:S(2)}) collective-permute-start(bf16[384,1024]{1,0:T(8,128)(2,1)} %get-tuple-element.146), channel_id=1, source_target_pairs={{0,32},{1,33},{2,34},{3,35},{4,36},{5,37},{6,38},{7,39},{8,40},{9,... | collective-permute-start | bytes 2359304 | tf_op jit(solution)/shard_map/ppermute | solution.py:31
  22.4 58.9 %collective-permute-start.2 = (bf16[384,1024]{1,0:T(8,128)(2,1)}, bf16[384,1024]{1,0:T(8,128)(2,1)}, u32[]{:S(2)}, u32[]{:S(2)}) collective-permute-start(bf16[384,1024]{1,0:T(8,128)(2,1)} %get-tuple-element.146), channel_id=1, source_target_pairs={{0,64},{1,65},{2,66},{3,67},{4,68},{5,69},{6,70},{7,71},{8,72},{9,... | collective-permute-start | bytes 2359304 | tf_op jit(solution)/shard_map/ppermute | solution.py:31
  25.0 54.2 %collective-permute-start.1 = (bf16[384,1024]{1,0:T(8,128)(2,1)}, bf16[384,1024]{1,0:T(8,128)(2,1)}, u32[]{:S(2)}, u32[]{:S(2)}) collective-permute-start(bf16[384,1024]{1,0:T(8,128)(2,1)} %get-tuple-element.146), channel_id=1, source_target_pairs={{1,0},{2,1},{3,2},{4,3},{5,4},{6,5},{7,6},{8,7},{9,8},{10,9},{11,1... | collective-permute-start | bytes 2359304 | tf_op jit(solution)/shard_map/ppermute | solution.py:23
  26.7 50.4 %collective-permute-start = (bf16[384,1024]{1,0:T(8,128)(2,1)}, bf16[384,1024]{1,0:T(8,128)(2,1)}, u32[]{:S(2)}, u32[]{:S(2)}) collective-permute-start(bf16[384,1024]{1,0:T(8,128)(2,1)} %get-tuple-element.146), channel_id=1, source_target_pairs={{0,1},{1,2},{2,3},{3,4},{4,5},{5,6},{6,7},{7,8},{8,9},{9,10},{10,1... | collective-permute-start | bytes 2359304 | tf_op jit(solution)/shard_map/ppermute | solution.py:20
  109.4 3.0 copy-start.1
  115.9 3.0 copy-start.8
  137.1 3.0 copy-start.1
  143.7 3.0 copy-start.8
  164.8 3.0 copy-start.1
  192.5 3.0 copy-start.1
  202.0 114.5 %slice-start = ((s8[4718592]{0:T(1024)(128)(4,1)}), s8[4194304]{0:T(1024)(128)(4,1)S(1)}, s32[]{:S(2)}) async-start(s8[4718592]{0:T(1024)(128)(4,1)} %bitcast.156), calls=%async_computation.1 | async-start | bytes 8388608
  202.0 114.6 %slice-start.2 = ((s8[4718592]{0:T(1024)(128)(4,1)}), s8[4194304]{0:T(1024)(128)(4,1)S(1)}, s32[]{:S(2)}) async-start(s8[4718592]{0:T(1024)(128)(4,1)} %bitcast.160), calls=%async_computation.3 | async-start | bytes 8388608
  202.0 16.7 %copy-start.10 = (bf16[1,384,512]{2,1,0:T(8,128)(2,1)S(1)}, bf16[1,384,512]{2,1,0:T(8,128)(2,1)}, u32[]{:S(2)}) copy-start(bf16[1,384,512]{2,1,0:T(8,128)(2,1)} %param.11) | copy-start | bytes 1179652
  202.0 16.7 %copy-start.11 = (bf16[4,384,128]{1,2,0:T(8,128)(2,1)S(1)}, bf16[4,384,128]{1,2,0:T(8,128)(2,1)}, u32[]{:S(2)}) copy-start(bf16[4,384,128]{1,2,0:T(8,128)(2,1)} %get-tuple-element.66) | copy-start | bytes 1179652
  202.0 18.2 %copy-start.5 = (f32[4,384,128]{1,2,0:T(8,128)S(1)}, f32[4,384,128]{1,2,0:T(8,128)}, u32[]{:S(2)}) copy-start(f32[4,384,128]{1,2,0:T(8,128)} %get-tuple-element.67) | copy-start | bytes 2359300
  202.0 114.5 %slice-start.1 = ((s8[4718592]{0:T(1024)(128)(4,1)}), s8[524288]{0:T(1024)(128)(4,1)S(1)}, s32[]{:S(2)}) async-start(s8[4718592]{0:T(1024)(128)(4,1)} %bitcast.156), calls=%async_computation.2 | async-start | bytes 1048576
  202.0 114.5 %slice-start.3 = ((s8[4718592]{0:T(1024)(128)(4,1)}), s8[524288]{0:T(1024)(128)(4,1)S(1)}, s32[]{:S(2)}) async-start(s8[4718592]{0:T(1024)(128)(4,1)} %bitcast.160), calls=%async_computation.4 | async-start | bytes 1048576
  208.0 108.5 %collective-permute-start.5 = (f32[384,1024]{0,1:T(8,128)}, f32[384,1024]{0,1:T(8,128)S(1)}, u32[]{:S(2)}, u32[]{:S(2)}) collective-permute-start(f32[384,1024]{0,1:T(8,128)} %get-tuple-element.136), channel_id=1, source_target_pairs={{0,1},{1,2},{2,3},{3,4},{4,5},{5,6},{6,7},{7,8},{8,9},{9,10},{10,1... | collective-permute-start | bytes 4718600 | tf_op jit(solution)/shard_map/ppermute | solution.py:20
  208.0 108.5 %collective-permute-start.6 = (f32[384,1024]{0,1:T(8,128)}, f32[384,1024]{0,1:T(8,128)S(1)}, u32[]{:S(2)}, u32[]{:S(2)}) collective-permute-start(f32[384,1024]{0,1:T(8,128)} %get-tuple-element.137), channel_id=1, source_target_pairs={{1,0},{2,1},{3,2},{4,3},{5,4},{6,5},{7,6},{8,7},{9,8},{10,9},{11,1... | collective-permute-start | bytes 4718600 | tf_op jit(solution)/shard_map/ppermute | solution.py:23
  214.9 101.6 %collective-permute-start.7 = (f32[384,1024]{0,1:T(8,128)}, f32[384,1024]{0,1:T(8,128)S(1)}, u32[]{:S(2)}, u32[]{:S(2)}) collective-permute-start(f32[384,1024]{0,1:T(8,128)} %get-tuple-element.138), channel_id=1, source_target_pairs={{0,64},{1,65},{2,66},{3,67},{4,68},{5,69},{6,70},{7,71},{8,72},{9,... | collective-permute-start | bytes 4718600 | tf_op jit(solution)/shard_map/ppermute | solution.py:31
  214.9 101.6 %collective-permute-start.9 = (f32[384,1024]{0,1:T(8,128)S(1)}, f32[384,1024]{0,1:T(8,128)S(1)}, u32[]{:S(2)}, u32[]{:S(2)}) collective-permute-start(f32[384,1024]{0,1:T(8,128)S(1)} %get-tuple-element.139), channel_id=1, source_target_pairs={{0,16},{1,17},{2,18},{3,19},{4,20},{5,21},{6,22},{7,23},{8,24},{9,... | collective-permute-start | bytes 4718600 | tf_op jit(solution)/shard_map/ppermute | solution.py:31
  218.3 98.2 %collective-permute-start.8 = (f32[384,1024]{0,1:T(8,128)S(1)}, f32[384,1024]{0,1:T(8,128)S(1)}, u32[]{:S(2)}, u32[]{:S(2)}) collective-permute-start(f32[384,1024]{0,1:T(8,128)S(1)} %get-tuple-element.140), channel_id=1, source_target_pairs={{0,32},{1,33},{2,34},{3,35},{4,36},{5,37},{6,38},{7,39},{8,40},{9,... | collective-permute-start | bytes 4718600 | tf_op jit(solution)/shard_map/ppermute | solution.py:31
  320.4 3.9 copy-start.3
  587.2 5.2 copy-start.13
  587.2 6.5 %copy-start.12 = (f32[512,512]{1,0:T(8,128)S(1)}, f32[512,512]{1,0:T(8,128)}, u32[]{:S(2)}) copy-start(f32[512,512]{1,0:T(8,128)} %get-tuple-element.276) | copy-start | bytes 3145732
  (7 other events, 12.6 us)
Sparse Core Ops, SparseCore 0:
  320.6 266.6 all-reduce.2
where the time goes:
time: 603 us; the launch traced here: 602 us
  waiting for transfers between devices  403 us (67%)
  local copies, waits for them, and re-layouts  68.6 us (11%)
  matrix products  66.2 us (11%)
  starting transfers between devices  24.1 us (4%)
  other arithmetic  21.8 us (4%)
  between operations  14.3 us (2%)
    psum x1, waiting for transfers between devices, per_device(): lax.psum((g_query, g_both[:, :width_all], g_both[:, width_all:], g_out),...  259 us
    ppermute x2, waiting for transfers between devices, with_halo(): lax.ppermute(lax.slice_in_dim(block, block.shape[dim] - width, None, axis...  144 us
    sub x4, matrix products, head_pair(): exp_vals = jnp.exp(scores - row_max)  28.3 us
    unnamed x41, local copies, waits for them, and re-layouts  18.1 us
    ppermute x6, starting transfers between devices, from_partner(): return lax.ppermute(value, axis, pairs)  15.5 us
    convert_element_type x4, other arithmetic, head_pair(): prob_bf = prob_f32.astype(jnp.bfloat16)  15.3 us
    while x28, local copies, waits for them, and re-layouts  14.3 us
  transfers between devices with their start and end apart: 11, of which 3 were waited for; matrix products, arithmetic and copies ran while one was open for 3% of the time, Pallas kernels for 0%

commit v1 on v0

v1 whole, which is shorter than its diff:
```python
import functools
import jax
import jax.numpy as jnp
from jax import lax
from jax.experimental import pallas as pl
from jax.experimental.pallas import tpu as pltpu
from jax.sharding import PartitionSpec as P

BF, F32 = jnp.bfloat16, jnp.float32

ROWS = 384
D = 512
CAND = 6
PAIRS = 4
WIDE = 768
LOG2E = 1.4426950408889634


def nn(a, b):
    return lax.dot_general(a, b, (((1,), (0,)), ((), ())), preferred_element_type=F32)


def nt(a, b):
    return lax.dot_general(a, b, (((1,), (1,)), ((), ())), preferred_element_type=F32)


def block_diag(pair):
    zero = jnp.zeros((64, ROWS), pair.dtype)
    top = jnp.concatenate([pair[:64], zero], 1)
    low = jnp.concatenate([zero, pair[64:]], 1)
    return jnp.concatenate([top, low], 0)


def corners(wide):
    return jnp.concatenate([wide[:64, :ROWS], wide[64:, ROWS:]], 0)


def pair_cols(p, width=128):
    return pl.ds(pl.multiple_of(p * width, width), width)


def prepare(r):
    for p in range(PAIRS):
        r.wkv[:, 256 * p : 256 * p + 128] = r.wk[:, 128 * p : 128 * p + 128]
        r.wkv[:, 256 * p + 128 : 256 * p + 256] = r.wv[:, 128 * p : 128 * p + 128]
    q_t = nn(r.x[0], r.wq[...]).astype(BF).T
    q_t = q_t * jnp.asarray(0.125, BF)
    go_t = nt(r.cot[...], r.wo[...]).astype(BF).T
    for p in range(PAIRS):
        r.qbd[p] = block_diag(q_t[128 * p : 128 * p + 128])
        r.gbd[p] = block_diag(go_t[128 * p : 128 * p + 128])
    r.m[...] = jnp.full_like(r.m, -3e38)
    r.l[...] = jnp.zeros_like(r.l)
    r.o[...] = jnp.zeros_like(r.o)


def project(r, j):
    kv = nn(r.x[j], r.wkv[...]).astype(BF)
    r.kv[j] = kv
    r.kvt[j] = kv.T
    r.xt[:, ROWS * j : ROWS * (j + 1)] = r.x[j].T


def forward(r, j):
    def body(p, _):
        k = r.kv[j, :, pl.ds(pl.multiple_of(p * 256, 256), 128)]
        s = nn(k, r.qbd[p])
        old = r.m[p, 7:8]
        new = old
        shifts = []
        for i in range(3):
            c = 3 * j + i
            top = jnp.max(s[128 * i : 128 * i + 128], axis=0, keepdims=True) + r.bias[c : c + 1]
            new = jnp.maximum(new, top)
        total = jnp.zeros_like(new)
        for i in range(3):
            c = 3 * j + i
            ex = jnp.exp(s[128 * i : 128 * i + 128] - (new - r.bias[c : c + 1]))
            total = total + jnp.sum(ex, axis=0, keepdims=True)
            r.e[p, j, 128 * i : 128 * i + 128] = ex.astype(BF)
        alpha = jnp.exp(old - new)
        r.m[p, 7:8] = new
        r.m[p, j : j + 1] = new
        r.l[p, 0:1] = r.l[p, 0:1] * alpha + total
        vt = r.kvt[j, pl.ds(pl.multiple_of(p * 256 + 128, 128), 128), :]
        r.o[p] = r.o[p] * alpha + nn(vt, r.e[p, j])
        return 0

    lax.fori_loop(0, PAIRS, body, 0)


def finish_forward(r):
    def body(p, _):
        inv = 1.0 / r.l[p, 0:1]
        o_wide = (r.o[p] * inv).astype(BF)
        delta = jnp.sum(r.gbd[p].astype(F32) * o_wide.astype(F32), axis=0, keepdims=True)
        r.l[p, 1:2] = inv
        r.l[p, 2:3] = delta
        o_pair = corners(o_wide)
        r.ot[pair_cols(p), :] = o_pair
        return 0

    lax.fori_loop(0, PAIRS, body, 0)
    r.att[...] = nn(r.ot[...].T, r.wo[...]).astype(BF)
    r.gw[3] = nn(r.ot[...], r.cot[...]).astype(r.gw.dtype)


def backward(r, p, j, gq):
    k_cols = pl.ds(pl.multiple_of(p * 256, 256), 128)
    v_cols = pl.ds(pl.multiple_of(p * 256 + 128, 128), 128)
    gp = nn(r.kv[j, :, v_cols], r.gbd[p])
    gs = (gp - r.l[p, 2:3]).astype(BF) * r.e[p, j]
    scale = jnp.exp(r.m[p, j : j + 1] - r.m[p, 7:8]) * r.l[p, 1:2]
    scaled_q = (r.qbd[p].astype(F32) * scale).astype(BF)
    scaled_g = (r.gbd[p].astype(F32) * scale).astype(BF)
    rows = pl.ds(ROWS * j, ROWS)
    r.gkv[rows, k_cols] = nt(gs, scaled_q).astype(BF)
    r.gkv[rows, v_cols] = nt(r.e[p, j], scaled_g).astype(BF)
    return gq + nn(r.kvt[j, k_cols, :], gs) * scale


def backward_pair(r, p):
    gq = jnp.zeros((128, WIDE), F32)
    for j in range(CAND):
        gq = backward(r, p, j, gq)
    gq_t = (corners(gq) * 0.125).astype(BF)
    r.gqt[pair_cols(p), :] = gq_t
    cols = pair_cols(p)
    r.gw[0, :, cols] = nt(r.xt[:, :ROWS], gq_t).astype(r.gw.dtype)
    both = nn(r.xt[...], r.gkv[:, pl.ds(pl.multiple_of(p * 256, 256), 256)])
    r.gw[1, :, cols] = both[:, :128].astype(r.gw.dtype)
    r.gw[2, :, cols] = both[:, 128:].astype(r.gw.dtype)


def give_back(r, j):
    return nt(r.gkv[ROWS * j : ROWS * (j + 1)], r.wkv[...])


class Refs:
    pass


NAMES_IN = ("x", "cot", "bias", "wq", "wk", "wv", "wo")
SCRATCH = dict(
    wkv=((D, 2 * D), BF),
    qbd=((PAIRS, 128, WIDE), BF),
    gbd=((PAIRS, 128, WIDE), BF),
    m=((PAIRS, 8, WIDE), F32),
    l=((PAIRS, 8, WIDE), F32),
    o=((PAIRS, 128, WIDE), F32),
    ot=((D, ROWS), BF),
    gqt=((D, ROWS), BF),
    kv=((CAND, ROWS, 2 * D), BF),
    kvt=((CAND, 2 * D, ROWS), BF),
    xt=((D, CAND * ROWS), BF),
    e=((PAIRS, CAND, ROWS, WIDE), BF),
    gkv=((CAND * ROWS, 2 * D), BF),
)


def attn_kernel(*refs):
    r = Refs()
    outs = ("att", "back", "own", "gw")
    for name, ref in zip(NAMES_IN + outs + tuple(SCRATCH), refs):
        setattr(r, name, ref)
    prepare(r)
    for j in range(CAND):
        project(r, j)
        forward(r, j)
    finish_forward(r)

    def body(p, _):
        backward_pair(r, p)
        return 0

    lax.fori_loop(0, PAIRS, body, 0)
    for j in range(1, CAND):
        r.back[j - 1] = give_back(r, j).astype(BF)
    r.own[...] = give_back(r, 0) + nt(r.gqt[...].T, r.wq[...])


def attention(x_all, cot, bias, wq, wk, wv, wo):
    vmem = pl.BlockSpec(memory_space=pltpu.VMEM)
    return pl.pallas_call(
        attn_kernel,
        out_shape=(
            jax.ShapeDtypeStruct((ROWS, D), BF),
            jax.ShapeDtypeStruct((CAND - 1, ROWS, D), BF),
            jax.ShapeDtypeStruct((ROWS, D), F32),
            jax.ShapeDtypeStruct((4, D, D), F32),
        ),
        in_specs=[vmem] * 7,
        out_specs=(vmem,) * 4,
        scratch_shapes=[pltpu.VMEM(s, d) for s, d in SCRATCH.values()],
        compiler_params=pltpu.CompilerParams(vmem_limit_bytes=60 * 1024 * 1024),
        name="attention",
    )(x_all, cot, bias, wq, wk, wv, wo)


def masking(tile_mask):
    own = jnp.arange(18)[None, :] == jnp.arange(3)[:, None]
    live = (tile_mask == 1) | own
    b = jnp.where(live, 0.0, -1e30).astype(F32).T
    b = jnp.repeat(b, 128, axis=1)
    return jnp.concatenate([b, b], 1)

MESH = pl.DeviceIdType.MESH
RING_X, RING_Y, RING_Z = (1, 4), (32, 4), (4, 8)
ORDER = ((RING_X, RING_Z, RING_Y), (RING_Y, RING_Z, RING_X))


def place(me, ring):
    stride, size = ring
    return lax.rem(me // stride, size)


def peer(me, ring, step):
    stride, size = ring
    at = place(me, ring)
    return me + (lax.rem(at + step, size) - at) * stride


def partners(me):
    return [lax.rem(me + 1, 128), lax.rem(me + 127, 128), me ^ 64, me ^ 32, me ^ 16]


def greet(me):
    barrier = pltpu.get_barrier_semaphore()
    peers = [peer(me, ring, s) for ring in (RING_X, RING_Y, RING_Z) for s in range(1, ring[1])]
    peers += partners(me)[:2]
    for p in peers:
        pl.semaphore_signal(barrier, inc=1, device_id={"dom": p}, device_id_type=MESH)
    other = 1 - lax.axis_index("dp")
    pl.semaphore_signal(barrier, inc=1, device_id={"dp": other}, device_id_type=MESH)
    pl.semaphore_wait(barrier, len(peers) + 1)


class Reduce:
    def __init__(self, r, me, core, chunk, start, width):
        self.r, self.me, self.core, self.chunk = r, me, core, chunk
        self.lanes = pl.ds(start, width)

    def copy(self, src, dst, color, stage, k, target):
        return pltpu.make_async_remote_copy(
            src_ref=src,
            dst_ref=dst,
            send_sem=self.r.send_sem.at[self.chunk, color, stage, k],
            recv_sem=self.r.recv_sem.at[self.chunk, color, stage, k],
            device_id=target,
            device_id_type=MESH,
        )

    def core_copy(self):
        return self.copy(
            self.r.give.at[:, self.lanes], self.r.got.at[:, self.lanes], 0, 5, 0,
            {"dp": 1 - self.core},
        )

    def first_copies(self, color):
        ring = ORDER[color][0]
        made = []
        for s in range(1, ring[1]):
            to = lax.rem(place(self.me, ring) + s, ring[1])
            made.append(self.copy(
                self.r.half.at[pl.ds(512 * color + to * 128, 128), self.lanes],
                self.r.slot1.at[color, s - 1, :, self.lanes], color, 0, s,
                {"dom": peer(self.me, ring, s)},
            ))
        return made

    def second_copies(self, color):
        ring = ORDER[color][1]
        made = []
        for s in range(1, ring[1]):
            to = lax.rem(place(self.me, ring) + s, ring[1])
            made.append(self.copy(
                self.r.part1.at[color, pl.ds(to * 16, 16), self.lanes],
                self.r.slot2.at[color, s - 1, :, self.lanes], color, 1, s,
                {"dom": peer(self.me, ring, s)},
            ))
        return made

    def third_copies(self, color):
        ring = ORDER[color][2]
        at = place(self.me, ring)
        spot = self.r.slot3.at[color, at, :, self.lanes]
        return [
            self.copy(spot, spot, color, 2, s, {"dom": peer(self.me, ring, s)})
            for s in range(1, ring[1])
        ]

    def result(self, color, row, count):
        return self.r.gw.at[2 * color + row // 256, self.core, pl.ds(lax.rem(row, 256), count), self.lanes]

    def fourth_copies(self, color):
        first, second, _ = ORDER[color]
        row = place(self.me, first) * 128 + place(self.me, second) * 16
        spot = self.result(color, row, 16)
        return [
            self.copy(spot, spot, color, 3, s, {"dom": peer(self.me, second, s)})
            for s in range(1, second[1])
        ]

    def fifth_copies(self, color):
        first = ORDER[color][0]
        spot = self.result(color, place(self.me, first) * 128, 128)
        return [
            self.copy(spot, spot, color, 4, s, {"dom": peer(self.me, first, s)})
            for s in range(1, first[1])
        ]

    def last_copy(self, color):
        spot = self.r.gw.at[pl.ds(2 * color, 2), self.core, :, self.lanes]
        return self.copy(spot, spot, color, 5, 1, {"dp": 1 - self.core})

    def step0(self):
        self.core_copy().start()

    def step1(self):
        self.core_copy().wait()
        r, lanes = self.r, self.lanes
        for b in range(8):
            rows = pl.ds(128 * b, 128)
            t = r.own_half[rows, lanes] + r.got[rows, lanes].astype(F32)
            r.own_half[rows, lanes] = t
            r.half[rows, lanes] = t.astype(BF)
            if b == 3:
                for c in self.first_copies(0):
                    c.start()
        for c in self.first_copies(1):
            c.start()

    def step2(self, color):
        r, lanes = self.r, self.lanes
        for c in self.first_copies(color):
            c.wait()
        at = place(self.me, ORDER[color][0])
        t = r.own_half[pl.ds(512 * color + at * 128, 128), lanes]
        for s in range(3):
            t = t + r.slot1[color, s, :, lanes].astype(F32)
        r.sum1[color, :, lanes] = t
        r.part1[color, :, lanes] = t.astype(BF)
        for c in self.second_copies(color):
            c.start()

    def step3(self, color):
        r, lanes = self.r, self.lanes
        for c in self.second_copies(color):
            c.wait()
        t = r.sum1[color, pl.ds(place(self.me, ORDER[color][1]) * 16, 16), lanes]
        for s in range(7):
            t = t + r.slot2[color, s, :, lanes].astype(F32)
        r.slot3[color, place(self.me, ORDER[color][2]), :, lanes] = t.astype(BF)
        for c in self.third_copies(color):
            c.start()

    def step4(self, color):
        r, lanes = self.r, self.lanes
        for c in self.third_copies(color):
            c.wait()
        t = r.slot3[color, 0, :, lanes].astype(F32)
        for s in range(1, 4):
            t = t + r.slot3[color, s, :, lanes].astype(F32)
        first, second, _ = ORDER[color]
        row = place(self.me, first) * 128 + place(self.me, second) * 16
        r.gw[2 * color + row // 256, self.core, pl.ds(lax.rem(row, 256), 16), lanes] = t.astype(BF)
        for c in self.fourth_copies(color):
            c.start()

    def step5(self, color):
        for c in self.fourth_copies(color):
            c.wait()
        for c in self.fifth_copies(color):
            c.start()

    def step6(self, color):
        for c in self.fifth_copies(color):
            c.wait()
        self.last_copy(color).start()

    def step7(self):
        for color in range(2):
            self.last_copy(color).wait()

    def run(self):
        self.step0()
        self.step1()
        for step in (self.step2, self.step3, self.step4, self.step5, self.step6):
            step(0)
            step(1)
        self.step7()


def reduce_scratch(chunks):
    return dict(
        give=pltpu.VMEM((1024, 512), BF),
        got=pltpu.VMEM((1024, 512), BF),
        own_half=pltpu.VMEM((1024, 512), F32),
        half=pltpu.VMEM((1024, 512), BF),
        slot1=pltpu.VMEM((2, 3, 128, 512), BF),
        sum1=pltpu.VMEM((2, 128, 512), F32),
        part1=pltpu.VMEM((2, 128, 512), BF),
        slot2=pltpu.VMEM((2, 7, 16, 512), BF),
        slot3=pltpu.VMEM((2, 4, 16, 512), BF),
        send_sem=pltpu.SemaphoreType.DMA((chunks, 2, 6, 8)),
        recv_sem=pltpu.SemaphoreType.DMA((chunks, 2, 6, 8)),
    )


def tail_kernel(names, *refs):
    r = Refs()
    for name, ref in zip(names, refs):
        setattr(r, name, ref)
    me, core = lax.axis_index("dom"), lax.axis_index("dp")
    greet(me)
    targets = [lax.rem(me + 127, 128), lax.rem(me + 1, 128), me ^ 64, me ^ 32, me ^ 16]
    back = []
    for j in (4, 2, 0, 1, 3):
        c = pltpu.make_async_remote_copy(
            src_ref=r.back.at[j], dst_ref=r.landed.at[j],
            send_sem=r.ret_send.at[j], recv_sem=r.ret_recv.at[j],
            device_id={"dom": targets[j]}, device_id_type=MESH,
        )
        c.start()
        back.append(c)
    for m in range(4):
        r.give[256 * m : 256 * m + 256] = r.part[m, 1 - core].astype(BF)
        r.own_half[256 * m : 256 * m + 256] = r.part[m, core]
    red = Reduce(r, me, core, 0, 0, 512)
    red.run()
    total = r.own[...]
    for c in back:
        c.wait()
    for j in range(5):
        total = total + r.landed[j].astype(F32)
    r.gx[...] = total.astype(BF)


def tail(back, own, part):
    vmem = pl.BlockSpec(memory_space=pltpu.VMEM)
    scratch = dict(
        landed=pltpu.VMEM((5, 384, 512), BF),
        ret_send=pltpu.SemaphoreType.DMA((5,)),
        ret_recv=pltpu.SemaphoreType.DMA((5,)),
        **reduce_scratch(1),
    )
    names = ("back", "own", "part", "gx", "gw") + tuple(scratch)
    return pl.pallas_call(
        functools.partial(tail_kernel, names),
        out_shape=(
            jax.ShapeDtypeStruct((384, 512), BF),
            jax.ShapeDtypeStruct((4, 2, 256, 512), BF),
        ),
        in_specs=[vmem] * 3,
        out_specs=(vmem,) * 2,
        scratch_shapes=list(scratch.values()),
        compiler_params=pltpu.CompilerParams(
            collective_id=1, has_side_effects=True, vmem_limit_bytes=40 * 1024 * 1024
        ),
        name="return_and_reduce",
    )(back, own, part.reshape(4, 2, 256, 512))


def spread_kernel(x_ref, all_ref, local_sem, send_sem, recv_sem):
    me = lax.axis_index("dom")
    targets = [lax.rem(me + 1, 128), lax.rem(me + 127, 128), me ^ 64, me ^ 32, me ^ 16]
    barrier = pltpu.get_barrier_semaphore()
    for t in targets:
        pl.semaphore_signal(barrier, inc=1, device_id={"dom": t}, device_id_type=MESH)
    pl.semaphore_wait(barrier, 5)
    copies = []
    for j in (4, 2, 0, 1, 3):
        c = pltpu.make_async_remote_copy(
            src_ref=x_ref, dst_ref=all_ref.at[j + 1], send_sem=send_sem.at[j], recv_sem=recv_sem.at[j],
            device_id={"dom": targets[j]}, device_id_type=MESH,
        )
        c.start()
        copies.append(c)
    all_ref[0] = x_ref[...]
    for c in copies:
        c.wait()


def spread(x):
    vmem = pl.BlockSpec(memory_space=pltpu.VMEM)
    return pl.pallas_call(
        spread_kernel,
        out_shape=jax.ShapeDtypeStruct((6, 384, 512), BF),
        in_specs=[vmem],
        out_specs=vmem,
        scratch_shapes=[pltpu.SemaphoreType.DMA, pltpu.SemaphoreType.DMA((5,)), pltpu.SemaphoreType.DMA((5,))],
        compiler_params=pltpu.CompilerParams(collective_id=0, has_side_effects=True),
        name="spread_features",
    )(x)
def per_device(features, tile_mask, cotangent, wq, wk, wv, wo):
    xall=spread(features[0])
    att,back,own,gw=attention(xall,cotangent[0],masking(tile_mask[0]),wq,wk,wv,wo)
    gx,gw=tail(back,own,gw)
    gw=gw.reshape(4,512,512).astype(F32)
    return att[None], gx[None], gw[0],gw[1],gw[2],gw[3]
def solution(mesh):
    s=P("dp","dom",None)
    return jax.shard_map(per_device,mesh=mesh,in_specs=(s,s,s,P(),P(),P(),P()),out_specs=(s,s,P(),P(),P(),P()),check_vma=False)
```

time: 603 us -> 163 us (0.27)
  waiting for transfers between devices: 403 us -> 0 us
  Pallas kernels: 0 us -> 153 us
  matrix products: 66.2 us -> 0 us
  local copies, waits for them, and re-layouts: 68.6 us -> 8.04 us
  starting transfers between devices: 24.1 us -> 0 us
  other arithmetic: 21.8 us -> 1.33 us
  between operations: 14.3 us -> 0.67 us
    psum x1 -> x0, waiting for transfers between devices: 259 us -> none  [per_device(): lax.psum((g_query, g_both[:, :width_all], g_both[:, width_all:], g_out),...]
    pallas_call x0 -> x3, Pallas kernels: none -> 153 us  [the longest x1 60.1 us: tail(): pl.pallas_call(functools.partial(tail_kernel, names), out_shape=(jax.Shap...]
    ppermute x10 -> x0, waiting for transfers between devices: 144 us -> none  [the longest x2 144 us: with_halo(): lax.ppermute(lax.slice_in_dim(block, block.shape[dim] - width, None, axis...]
    dot_general x29 -> x0, matrix products: 37.9 us -> none  [the longest x4 6.58 us: head_pair(): jnp.einsum('rhd,chd->hrc', g_pair, v_pair, preferred_element_type=jnp.flo...]
    sub x4 -> x0, matrix products: 28.3 us -> none  [head_pair(): exp_vals = jnp.exp(scores - row_max)]
    ppermute x10 -> x0, starting transfers between devices: 24.1 us -> none  [the longest x6 15.5 us: from_partner(): return lax.ppermute(value, axis, pairs)]
    convert_element_type x4 -> x0, other arithmetic: 15.3 us -> none  [head_pair(): prob_bf = prob_f32.astype(jnp.bfloat16)]
    dynamic_slice x36 -> x0, local copies, waits for them, and re-layouts: 14.6 us -> none  [the longest x8 5.43 us: head_pair(): lax.dynamic_slice_in_dim(keys_all, col_start, pair_cols, 1)]
  transfers between devices with their start and end apart: 11 -> 0, of which waited for: 3 -> 0; matrix products, arithmetic and copies ran while one was open for 3% -> 0% of each run, Pallas kernels for 0% -> 0%
where the time goes in v1:
time: 163 us
  Pallas kernels  153 us (94%)
  local copies, waits for them, and re-layouts  8.04 us (5%)
    pallas_call x1, Pallas kernels, tail(): pl.pallas_call(functools.partial(tail_kernel, names), out_shape=(jax.Shap...  60.1 us
    pallas_call x1, Pallas kernels, attention(): pl.pallas_call(attn_kernel, out_shape=(jax.ShapeDtypeStruct((ROWS, D), BF...  51.7 us
    pallas_call x1, Pallas kernels, spread(): pl.pallas_call(spread_kernel, out_shape=jax.ShapeDtypeStruct((6, 384, 512...  40.9 us
    unnamed x9, local copies, waits for them, and re-layouts  5.63 us

profile of v1, /device:TPU:1, one launch (start us, length us, event | category | flops | bytes accessed | tf_op | source)
XLA Modules:
  0.0 162.7 jit_solution(11229543654343986664)
XLA Ops:
  0.6 0.7 broadcast_compare_fusion
  1.3 0.1 copy.13
  1.4 0.1 broadcast_in_dim.21
  1.5 0.6 pad_maximum_fusion.refs_2_
  2.2 40.9 %spread_features.1.refs_0_ = bf16[6,384,512]{2,1,0:T(8,128)(2,1)} custom-call(bf16[384,512]{1,0:T(8,128)(2,1)} %bitcast.23), custom_call_target="tpu_custom_call" | custom-call | tf_op jit(solution)/shard_map/spread_features/pallas_call | solution.py:486
  43.1 51.7 %attention.1 = (bf16[384,512]{1,0:T(8,128)(2,1)}, bf16[5,384,512]{2,1,0:T(8,128)(2,1)}, f32[384,512]{1,0:T(8,128)}, f32[4,512,512]{2,1,0:T(8,128)}) custom-call(bf16[6,384,512]{2,1,0:T(8,128)(2,1)} %spread_features.1.refs_0_, bf16[384,512]{1,0:T(8,128)(2,1)} %bitcast.22, f32[18,768]{1,0:T(8,128)} %pad_maximum_fusion.refs_2_, bf16[512,512]{1,0:T(8,128)(2,1)} %refs_3_.1, ...), custom_call_target="tpu_custom_call" | custom-call | tf_op jit(solution)/shard_map/attention/pallas_call | solution.py:184
  94.8 0.0 copy-start
  94.8 2.2 %copy-done = f32[4,512,512]{2,1,0:T(8,128)S(1)} copy-done((f32[4,512,512]{2,1,0:T(8,128)S(1)}, f32[4,512,512]{2,1,0:T(8,128)}, u32[]{:S(2)}) %copy-start) | copy-done | bytes 4194328
  97.0 0.0 copy-start.1
  97.0 1.5 copy-done.1
  98.5 0.0 copy-start.2
  98.5 1.1 copy-done.2
  99.6 60.1 %return_and_reduce.1 = (bf16[384,512]{1,0:T(8,128)(2,1)S(1)}, bf16[4,2,256,512]{3,2,1,0:T(8,128)(2,1)S(1)}) custom-call(bf16[5,384,512]{2,1,0:T(8,128)(2,1)S(1)} %copy-done.1, f32[384,512]{1,0:T(8,128)S(1)} %copy-done.2, f32[4,2,256,512]{3,2,1,0:T(8,128)S(1)} %bitcast.16), custom_call_target="tpu_custom_call" | custom-call | tf_op jit(solution)/shard_map/return_and_reduce/pallas_call | solution.py:448
  159.7 2.2 %fusion.1 = (f32[1,2,256,512]{3,2,1,0:T(8,128)}, f32[1,2,256,512]{3,2,1,0:T(8,128)}, f32[1,2,256,512]{3,2,1,0:T(8,128)}, f32[1,2,256,512]{3,2,1,0:T(8,128)}) fusion(bf16[4,2,256,512]{3,2,1,0:T(8,128)(2,1)S(1)} %get-tuple-element.17), kind=kLoop, calls=%fused_computation.5 | loop fusion | bytes 8388608 | tf_op jit(solution)/shard_map/slice | solution.py:500
  162.0 0.7 copy.18
  (3 shorter events, 0.0 us)
Async XLA Ops:
  94.8 2.2 %copy-start = (f32[4,512,512]{2,1,0:T(8,128)S(1)}, f32[4,512,512]{2,1,0:T(8,128)}, u32[]{:S(2)}) copy-start(f32[4,512,512]{2,1,0:T(8,128)} %get-tuple-element.15) | copy-start | bytes 12582916
  97.0 1.5 copy-start.1
  98.5 1.1 copy-start.2

commit v2 on v1

--- a/solution.py
+++ b/solution.py
@@ -39,10 +39,16 @@
     return pl.ds(pl.multiple_of(p * width, width), width)
 
 
+def load_copies(r):
+    made = [(r.x_hbm, r.x.at[0]), (r.cot_hbm, r.cot), (r.wq_hbm, r.wq), (r.wo_hbm, r.wo)]
+    for p in range(PAIRS):
+        cols = pl.ds(128 * p, 128)
+        made.append((r.wk_hbm.at[:, cols], r.wkv.at[:, pl.ds(256 * p, 128)]))
+        made.append((r.wv_hbm.at[:, cols], r.wkv.at[:, pl.ds(256 * p + 128, 128)]))
+    return [pltpu.make_async_copy(a, b, r.load_sem.at[i]) for i, (a, b) in enumerate(made)]
+
+
 def prepare(r):
-    for p in range(PAIRS):
-        r.wkv[:, 256 * p : 256 * p + 128] = r.wk[:, 128 * p : 128 * p + 128]
-        r.wkv[:, 256 * p + 128 : 256 * p + 256] = r.wv[:, 128 * p : 128 * p + 128]
     q_t = nn(r.x[0], r.wq[...]).astype(BF).T
     q_t = q_t * jnp.asarray(0.125, BF)
     go_t = nt(r.cot[...], r.wo[...]).astype(BF).T
@@ -86,7 +92,7 @@
         r.o[p] = r.o[p] * alpha + nn(vt, r.e[p, j])
         return 0
 
-    lax.fori_loop(0, PAIRS, body, 0)
+    lax.fori_loop(0, PAIRS, body, 0, unroll=True)
 
 
 def finish_forward(r):
@@ -102,10 +108,16 @@
 
     lax.fori_loop(0, PAIRS, body, 0)
     r.att[...] = nn(r.ot[...].T, r.wo[...]).astype(BF)
-    r.gw[3] = nn(r.ot[...], r.cot[...]).astype(r.gw.dtype)
-
-
-def backward(r, p, j, gq):
+    put(r, 3, 0, nn(r.ot[...], r.cot[...]))
+
+
+def put(r, m, start, value):
+    cols = pl.ds(start, value.shape[1])
+    r.part[m, 0, :, cols] = value[:256]
+    r.part[m, 1, :, cols] = value[256:]
+
+
+def backward(r, p, j, first):
     k_cols = pl.ds(pl.multiple_of(p * 256, 256), 128)
     v_cols = pl.ds(pl.multiple_of(p * 256 + 128, 128), 128)
     gp = nn(r.kv[j, :, v_cols], r.gbd[p])
@@ -116,20 +128,18 @@
     rows = pl.ds(ROWS * j, ROWS)
     r.gkv[rows, k_cols] = nt(gs, scaled_q).astype(BF)
     r.gkv[rows, v_cols] = nt(r.e[p, j], scaled_g).astype(BF)
-    return gq + nn(r.kvt[j, k_cols, :], gs) * scale
-
-
-def backward_pair(r, p):
-    gq = jnp.zeros((128, WIDE), F32)
-    for j in range(CAND):
-        gq = backward(r, p, j, gq)
-    gq_t = (corners(gq) * 0.125).astype(BF)
+    gq = nn(r.kvt[j, k_cols, :], gs) * scale
+    r.o[p] = gq if first else r.o[p] + gq
+
+
+def finish_pair(r, p):
+    gq_t = (corners(r.o[p]) * 0.125).astype(BF)
     r.gqt[pair_cols(p), :] = gq_t
-    cols = pair_cols(p)
-    r.gw[0, :, cols] = nt(r.xt[:, :ROWS], gq_t).astype(r.gw.dtype)
+    start = p * 128 if isinstance(p, int) else pl.multiple_of(p * 128, 128)
+    put(r, 0, start, nt(r.xt[:, :ROWS], gq_t))
     both = nn(r.xt[...], r.gkv[:, pl.ds(pl.multiple_of(p * 256, 256), 256)])
-    r.gw[1, :, cols] = both[:, :128].astype(r.gw.dtype)
-    r.gw[2, :, cols] = both[:, 128:].astype(r.gw.dtype)
+    put(r, 1, start, both[:, :128])
+    put(r, 2, start, both[:, 128:])
 
 
 def give_back(r, j):
@@ -140,7 +150,6 @@
     pass
 
 
-NAMES_IN = ("x", "cot", "bias", "wq", "wk", "wv", "wo")
 SCRATCH = dict(
     wkv=((D, 2 * D), BF),
     qbd=((PAIRS, 128, WIDE), BF),
@@ -155,54 +164,28 @@
     xt=((D, CAND * ROWS), BF),
     e=((PAIRS, CAND, ROWS, WIDE), BF),
     gkv=((CAND * ROWS, 2 * D), BF),
+    x=((CAND, ROWS, D), BF),
+    bias=((3 * CAND, WIDE), F32),
+    cot=((ROWS, D), BF),
+    wq=((D, D), BF),
+    wo=((D, D), BF),
+    att=((ROWS, D), BF),
+    gx=((ROWS, D), BF),
+    own=((ROWS, D), F32),
+    back=((CAND - 1, ROWS, D), BF),
+    landed=((CAND - 1, ROWS, D), BF),
+    part=((4, 2, 256, D), F32),
 )
 
 
-def attn_kernel(*refs):
-    r = Refs()
-    outs = ("att", "back", "own", "gw")
-    for name, ref in zip(NAMES_IN + outs + tuple(SCRATCH), refs):
-        setattr(r, name, ref)
-    prepare(r)
-    for j in range(CAND):
-        project(r, j)
-        forward(r, j)
-    finish_forward(r)
-
-    def body(p, _):
-        backward_pair(r, p)
-        return 0
-
-    lax.fori_loop(0, PAIRS, body, 0)
-    for j in range(1, CAND):
-        r.back[j - 1] = give_back(r, j).astype(BF)
-    r.own[...] = give_back(r, 0) + nt(r.gqt[...].T, r.wq[...])
-
-
-def attention(x_all, cot, bias, wq, wk, wv, wo):
-    vmem = pl.BlockSpec(memory_space=pltpu.VMEM)
-    return pl.pallas_call(
-        attn_kernel,
-        out_shape=(
-            jax.ShapeDtypeStruct((ROWS, D), BF),
-            jax.ShapeDtypeStruct((CAND - 1, ROWS, D), BF),
-            jax.ShapeDtypeStruct((ROWS, D), F32),
-            jax.ShapeDtypeStruct((4, D, D), F32),
-        ),
-        in_specs=[vmem] * 7,
-        out_specs=(vmem,) * 4,
-        scratch_shapes=[pltpu.VMEM(s, d) for s, d in SCRATCH.values()],
-        compiler_params=pltpu.CompilerParams(vmem_limit_bytes=60 * 1024 * 1024),
-        name="attention",
-    )(x_all, cot, bias, wq, wk, wv, wo)
-
-
-def masking(tile_mask):
-    own = jnp.arange(18)[None, :] == jnp.arange(3)[:, None]
-    live = (tile_mask == 1) | own
-    b = jnp.where(live, 0.0, -1e30).astype(F32).T
-    b = jnp.repeat(b, 128, axis=1)
-    return jnp.concatenate([b, b], 1)
+def masking(r):
+    for c in range(3 * CAND):
+        for t in range(3):
+            value = jnp.float32(0.0) if c == t else jnp.where(r.mask[t, c] == 1, 0.0, -1e30)
+            row = jnp.full((1, 128), value, F32)
+            r.bias[c : c + 1, 128 * t : 128 * t + 128] = row
+            r.bias[c : c + 1, ROWS + 128 * t : ROWS + 128 * t + 128] = row
+
 
 MESH = pl.DeviceIdType.MESH
 RING_X, RING_Y, RING_Z = (1, 4), (32, 4), (4, 8)
@@ -314,6 +297,9 @@
         return self.copy(spot, spot, color, 5, 1, {"dp": 1 - self.core})
 
     def step0(self):
+        r, lanes = self.r, self.lanes
+        for m in range(4):
+            r.give[256 * m : 256 * m + 256, lanes] = r.part[m, 1 - self.core, :, lanes].astype(BF)
         self.core_copy().start()
 
     def step1(self):
@@ -321,8 +307,9 @@
         r, lanes = self.r, self.lanes
         for b in range(8):
             rows = pl.ds(128 * b, 128)
-            t = r.own_half[rows, lanes] + r.got[rows, lanes].astype(F32)
-            r.own_half[rows, lanes] = t
+            t = r.part[b // 2, self.core, 128 * (b % 2) : 128 * (b % 2) + 128, lanes]
+            t = t + r.got[rows, lanes].astype(F32)
+            r.part[b // 2, self.core, 128 * (b % 2) : 128 * (b % 2) + 128, lanes] = t
             r.half[rows, lanes] = t.astype(BF)
             if b == 3:
                 for c in self.first_copies(0):
@@ -335,7 +322,7 @@
         for c in self.first_copies(color):
             c.wait()
         at = place(self.me, ORDER[color][0])
-        t = r.own_half[pl.ds(512 * color + at * 128, 128), lanes]
+        t = r.part[2 * color + at // 2, self.core, pl.ds(lax.rem(at, 2) * 128, 128), lanes]
         for s in range(3):
             t = t + r.slot1[color, s, :, lanes].astype(F32)
         r.sum1[color, :, lanes] = t
@@ -382,20 +369,17 @@
         for color in range(2):
             self.last_copy(color).wait()
 
-    def run(self):
-        self.step0()
-        self.step1()
-        for step in (self.step2, self.step3, self.step4, self.step5, self.step6):
-            step(0)
-            step(1)
-        self.step7()
+    def steps(self):
+        both = [self.step2, self.step3, self.step4, self.step5, self.step6]
+        made = [[self.step0], [self.step1]]
+        made += [[functools.partial(step, 0), functools.partial(step, 1)] for step in both]
+        return made + [[self.step7]]
 
 
 def reduce_scratch(chunks):
     return dict(
         give=pltpu.VMEM((1024, 512), BF),
         got=pltpu.VMEM((1024, 512), BF),
-        own_half=pltpu.VMEM((1024, 512), F32),
         half=pltpu.VMEM((1024, 512), BF),
         slot1=pltpu.VMEM((2, 3, 128, 512), BF),
         sum1=pltpu.VMEM((2, 128, 512), F32),
@@ -407,97 +391,131 @@
     )
 
 
-def tail_kernel(names, *refs):
+CHUNKS = ((0, 512),)
+ARRIVALS = (4, 1, 2, 3, 5)
+SENDS = (5, 3, 1, 2, 4)
+
+
+def layer_kernel(names, *refs):
     r = Refs()
     for name, ref in zip(names, refs):
         setattr(r, name, ref)
     me, core = lax.axis_index("dom"), lax.axis_index("dp")
+    before, after = lax.rem(me + 127, 128), lax.rem(me + 1, 128)
+    sources = (me, before, after, me ^ 64, me ^ 32, me ^ 16)
+    holders = (me, after, before, me ^ 64, me ^ 32, me ^ 16)
+    loads = load_copies(r)
+    for c in loads:
+        c.start()
     greet(me)
-    targets = [lax.rem(me + 127, 128), lax.rem(me + 1, 128), me ^ 64, me ^ 32, me ^ 16]
-    back = []
-    for j in (4, 2, 0, 1, 3):
-        c = pltpu.make_async_remote_copy(
-            src_ref=r.back.at[j], dst_ref=r.landed.at[j],
+    spread = {
+        j: pltpu.make_async_remote_copy(
+            src_ref=r.x_hbm, dst_ref=r.x.at[j], send_sem=r.fwd_send.at[j], recv_sem=r.fwd_recv.at[j],
+            device_id={"dom": holders[j]}, device_id_type=MESH,
+        )
+        for j in SENDS
+    }
+    returns = {
+        j: pltpu.make_async_remote_copy(
+            src_ref=r.back.at[j - 1], dst_ref=r.landed.at[j - 1],
             send_sem=r.ret_send.at[j], recv_sem=r.ret_recv.at[j],
-            device_id={"dom": targets[j]}, device_id_type=MESH,
+            device_id={"dom": sources[j]}, device_id_type=MESH,
         )
-        c.start()
-        back.append(c)
-    for m in range(4):
-        r.give[256 * m : 256 * m + 256] = r.part[m, 1 - core].astype(BF)
-        r.own_half[256 * m : 256 * m + 256] = r.part[m, core]
-    red = Reduce(r, me, core, 0, 0, 512)
-    red.run()
+        for j in SENDS
+    }
+    for j in ARRIVALS:
+        spread[j].start()
+    masking(r)
+    for c in loads:
+        c.wait()
+    prepare(r)
+    project(r, 0)
+    forward(r, 0)
+    for j in ARRIVALS:
+        spread[j].wait_recv()
+        project(r, j)
+        forward(r, j)
+    finish_forward(r)
+    out = pltpu.make_async_copy(r.att, r.att_hbm, r.out_sem.at[0])
+    out.start()
+
+    for i, j in enumerate(SENDS + (0,)):
+
+        def body(p, _, i=i, j=j):
+            backward(r, p, j, i == 0)
+            return 0
+
+        lax.fori_loop(0, PAIRS, body, 0, unroll=2)
+        if j:
+            r.back[j - 1] = give_back(r, j).astype(BF)
+            returns[j].start()
+
+    def finish(p, _):
+        finish_pair(r, p)
+        return 0
+
+    lax.fori_loop(0, PAIRS, finish, 0)
+    chunks = [Reduce(r, me, core, i, *c).steps() for i, c in enumerate(CHUNKS)]
+    running = [chunks[0]]
+
+    def advance():
+        for left in running:
+            if left:
+                for step in left.pop(0):
+                    step()
+
+    advance()
+    running += chunks[1:]
+    r.own[...] = give_back(r, 0) + nt(r.gqt[...].T, r.wq[...])
+    advance()
+    advance()
     total = r.own[...]
-    for c in back:
-        c.wait()
-    for j in range(5):
-        total = total + r.landed[j].astype(F32)
+    for j in SENDS:
+        returns[j].wait()
+        total = total + r.landed[j - 1].astype(F32)
     r.gx[...] = total.astype(BF)
-
-
-def tail(back, own, part):
+    out_x = pltpu.make_async_copy(r.gx, r.gx_hbm, r.out_sem.at[1])
+    out_x.start()
+    while any(running):
+        advance()
+    for j in SENDS:
+        spread[j].wait_send()
+    out.wait()
+    out_x.wait()
+
+
+def layer(x, cot, mask, wq, wk, wv, wo):
     vmem = pl.BlockSpec(memory_space=pltpu.VMEM)
-    scratch = dict(
-        landed=pltpu.VMEM((5, 384, 512), BF),
-        ret_send=pltpu.SemaphoreType.DMA((5,)),
-        ret_recv=pltpu.SemaphoreType.DMA((5,)),
-        **reduce_scratch(1),
-    )
-    names = ("back", "own", "part", "gx", "gw") + tuple(scratch)
+    hbm = pl.BlockSpec(memory_space=pl.ANY)
+    scratch = {name: pltpu.VMEM(s, d) for name, (s, d) in SCRATCH.items()}
+    scratch.update(reduce_scratch(len(CHUNKS)))
+    for name, count in dict(load_sem=12, fwd_send=6, fwd_recv=6, ret_send=6, ret_recv=6, out_sem=2).items():
+        scratch[name] = pltpu.SemaphoreType.DMA((count,))
+    names = ("x_hbm", "cot_hbm", "mask", "wq_hbm", "wk_hbm", "wv_hbm", "wo_hbm")
+    names += ("att_hbm", "gx_hbm", "gw") + tuple(scratch)
+    rows = jax.ShapeDtypeStruct((ROWS, D), BF)
     return pl.pallas_call(
-        functools.partial(tail_kernel, names),
-        out_shape=(
-            jax.ShapeDtypeStruct((384, 512), BF),
-            jax.ShapeDtypeStruct((4, 2, 256, 512), BF),
-        ),
-        in_specs=[vmem] * 3,
-        out_specs=(vmem,) * 2,
+        functools.partial(layer_kernel, names),
+        out_shape=(rows, rows, jax.ShapeDtypeStruct((4, 2, 256, D), BF)),
+        in_specs=[hbm, hbm, pl.BlockSpec(memory_space=pltpu.SMEM), hbm, hbm, hbm, hbm],
+        out_specs=(hbm, hbm, vmem),
         scratch_shapes=list(scratch.values()),
         compiler_params=pltpu.CompilerParams(
-            collective_id=1, has_side_effects=True, vmem_limit_bytes=40 * 1024 * 1024
+            collective_id=0, has_side_effects=True, vmem_limit_bytes=58 * 1024 * 1024
         ),
-        name="return_and_reduce",
-    )(back, own, part.reshape(4, 2, 256, 512))
-
-
-def spread_kernel(x_ref, all_ref, local_sem, send_sem, recv_sem):
-    me = lax.axis_index("dom")
-    targets = [lax.rem(me + 1, 128), lax.rem(me + 127, 128), me ^ 64, me ^ 32, me ^ 16]
-    barrier = pltpu.get_barrier_semaphore()
-    for t in targets:
-        pl.semaphore_signal(barrier, inc=1, device_id={"dom": t}, device_id_type=MESH)
-    pl.semaphore_wait(barrier, 5)
-    copies = []
-    for j in (4, 2, 0, 1, 3):
-        c = pltpu.make_async_remote_copy(
-            src_ref=x_ref, dst_ref=all_ref.at[j + 1], send_sem=send_sem.at[j], recv_sem=recv_sem.at[j],
-            device_id={"dom": targets[j]}, device_id_type=MESH,
-        )
-        c.start()
-        copies.append(c)
-    all_ref[0] = x_ref[...]
-    for c in copies:
-        c.wait()
-
-
-def spread(x):
-    vmem = pl.BlockSpec(memory_space=pltpu.VMEM)
-    return pl.pallas_call(
-        spread_kernel,
-        out_shape=jax.ShapeDtypeStruct((6, 384, 512), BF),
-        in_specs=[vmem],
-        out_specs=vmem,
-        scratch_shapes=[pltpu.SemaphoreType.DMA, pltpu.SemaphoreType.DMA((5,)), pltpu.SemaphoreType.DMA((5,))],
-        compiler_params=pltpu.CompilerParams(collective_id=0, has_side_effects=True),
-        name="spread_features",
-    )(x)
+        name="attention_layer",
+    )(x, cot, mask, wq, wk, wv, wo)
+
+
 def per_device(features, tile_mask, cotangent, wq, wk, wv, wo):
-    xall=spread(features[0])
-    att,back,own,gw=attention(xall,cotangent[0],masking(tile_mask[0]),wq,wk,wv,wo)
-    gx,gw=tail(back,own,gw)
-    gw=gw.reshape(4,512,512).astype(F32)
-    return att[None], gx[None], gw[0],gw[1],gw[2],gw[3]
+    att, gx, gw = layer(features[0], cotangent[0], tile_mask[0], wq, wk, wv, wo)
+    gw = gw.reshape(4, D, D).astype(F32)
+    return att[None], gx[None], gw[0], gw[1], gw[2], gw[3]
+
+
 def solution(mesh):
-    s=P("dp","dom",None)
-    return jax.shard_map(per_device,mesh=mesh,in_specs=(s,s,s,P(),P(),P(),P()),out_specs=(s,s,P(),P(),P(),P()),check_vma=False)
+    s = P("dp", "dom", None)
+    return jax.shard_map(
+        per_device, mesh=mesh, in_specs=(s, s, s, P(), P(), P(), P()),
+        out_specs=(s, s, P(), P(), P(), P()), check_vma=False,
+    )

time: 163 us -> 125 us (0.77)
  Pallas kernels: 153 us -> 117 us
    pallas_call x3 -> x1, Pallas kernels: 153 us -> 117 us  [layer(): pl.pallas_call(functools.partial(layer_kernel, names), out_shape=(rows, r...]
    unnamed x9 -> x7, local copies, waits for them, and re-layouts: 5.63 us -> 2.76 us
where the time goes in v2:
time: 125 us
  Pallas kernels  117 us (94%)
  local copies, waits for them, and re-layouts  6.58 us (5%)
    pallas_call x1, Pallas kernels, layer(): pl.pallas_call(functools.partial(layer_kernel, names), out_shape=(rows, r...  117 us
    slice x1, local copies, waits for them, and re-layouts, per_device(): return (att[None], gx[None], gw[0], gw[1], gw[2], gw[3])  3.82 us
    unnamed x7, local copies, waits for them, and re-layouts  2.76 us

profile of v2, /device:TPU:1, one launch (start us, length us, event | category | flops | bytes accessed | tf_op | source)
XLA Modules:
  0.0 124.6 jit_solution(16497089337841877040)
XLA Ops:
  0.6 1.3 %copy.15 = s32[1,3,18]{2,1,0:T(4,128)} copy(s32[1,3,18]{2,0,1:T(1,128)} %param.8) | data formatting | bytes 432
  1.9 117.4 %attention_layer.1 = (bf16[384,512]{1,0:T(8,128)(2,1)}, bf16[384,512]{1,0:T(8,128)(2,1)}, bf16[4,2,256,512]{3,2,1,0:T(8,128)(2,1)}) custom-call(bf16[384,512]{1,0:T(8,128)(2,1)} %bitcast.15, bf16[384,512]{1,0:T(8,128)(2,1)} %bitcast.16, s32[3,18]{1,0:T(4,128)} %bitcast.19, bf16[512,512]{1,0:T(8,128)(2,1)} %refs_3_.1, bf16[512,512]{1,0:T(8,128)(2,1)} %refs_4_.1, ...), custom_call_target="tpu_custom_call" | custom-call | tf_op jit(solution)/shard_map/attention_layer/pallas_call | solution.py:497
  119.3 0.0 copy-start.1
  119.3 0.0 copy-start
  119.3 3.8 %fusion = (f32[1,2,256,512]{3,2,1,0:T(8,128)}, f32[1,2,256,512]{3,2,1,0:T(8,128)}, f32[1,2,256,512]{3,2,1,0:T(8,128)}, f32[1,2,256,512]{3,2,1,0:T(8,128)}) fusion(bf16[4,2,256,512]{3,2,1,0:T(8,128)(2,1)} %get-tuple-element.11), kind=kLoop, calls=%fused_computation.1 | loop fusion | bytes 8388608 | tf_op jit(solution)/shard_map/slice | solution.py:513
  123.1 0.0 copy-done.1
  123.1 0.7 copy.18
  123.9 0.0 copy-done
  123.9 0.7 copy.19
Async XLA Ops:
  119.3 3.8 %copy-start.1 = (bf16[384,512]{1,0:T(8,128)(2,1)S(1)}, bf16[384,512]{1,0:T(8,128)(2,1)}, u32[]{:S(2)}) copy-start(bf16[384,512]{1,0:T(8,128)(2,1)} %get-tuple-element.9) | copy-start | bytes 1179652
  119.3 4.6 %copy-start = (bf16[384,512]{1,0:T(8,128)(2,1)S(1)}, bf16[384,512]{1,0:T(8,128)(2,1)}, u32[]{:S(2)}) copy-start(bf16[384,512]{1,0:T(8,128)(2,1)} %get-tuple-element.10) | copy-start | bytes 1179652
